TPU v7x, 512 devices: a whole 4x4x16 slice. The times are simulated.
512 devices in a mesh: row: 32 (over z_lo, x, core), col: 16 (over z_hi, y).
Axes of the slice: x: 4, y: 4, z: 16 (z_hi: 4, z_lo: 4; z = z_hi * 4 + z_lo), core: 2. Of those that a mesh axis runs over, the one named last changes fastest.
Arguments:
- vectors: bfloat16 [8, 262144], P(None, ('row', 'col')), may hold values from -6 to 6
- block_count: int32 [32, 16], P('row', 'col'), may hold values from 32 to 64, as said below
- block_index: int32 [32, 16, 2, 64], P('row', 'col'), may hold values from 0 to 63, as said below
- blocks: bfloat16 [32, 16, 64, 128, 128], P('row', 'col'), may hold values from -0.0625 to 0.0625
Outputs:
- applied: float32 [8, 262144], P(None, ('row', 'col'))
Inputs may be any that keep to these rules, and one draw needn't show every extreme that they name: `block_count`: some grid place has exactly 64 live slots. `block_index`: at grid column 0 each slot's block row is at most its block column. Slots beyond the live count hold indices too.
All inputs are finite; a program needn't handle non-finite values.
Results may differ from a plain program's by a relative error of at most 0.0003.
Values may be sent and summed in bfloat16 or wider, within the bound.
No kernel may reach another device: no remote copies, remote signals or barrier semaphores. Data moves between devices by JAX's collectives and lax.ppermute only.
A program may use at most 64 MiB of HBM per device.

v0:
```python
import jax
import jax.numpy as jnp
from jax import lax
from jax.sharding import PartitionSpec as P


def from_behind(value, axis, steps):
    count = lax.axis_size(axis)
    pairs = [(source, (source + steps) % count) for source in range(count)]
    return lax.ppermute(value, axis, pairs)


def per_device(vectors, block_count, block_index, blocks):
    col_count = lax.axis_size("col")
    col_place = lax.axis_index("col")
    home_seg = lax.all_gather(vectors, "col", axis=1, tiled=True)
    nvec, seg_len = home_seg.shape
    block_size = blocks.shape[-1]
    seg_blocks = seg_len // block_size
    levels = col_count.bit_length() - 1
    other_seg = home_seg
    for step_bit in range(levels):
        arrived = from_behind(other_seg, "row", -(1 << step_bit))
        other_seg = jnp.where((col_place >> step_bit) % 2 == 1, arrived, other_seg)
    live_count = block_count[0, 0]
    indices = block_index[0, 0]
    matrices = blocks[0, 0]
    slot_count = matrices.shape[0]
    active = jnp.arange(slot_count, dtype=jnp.int32) < live_count
    mirror = active & ((indices[0] != indices[1]) | (col_place != 0))
    places = jnp.arange(seg_blocks, dtype=jnp.int32)
    row_hot = indices[0][:, None] == places[None, :]
    col_hot = indices[1][:, None] == places[None, :]
    far_blocks = other_seg.reshape(nvec, seg_blocks, block_size)
    near_blocks = home_seg.reshape(nvec, seg_blocks, block_size)
    picked_far = jnp.einsum(
        "ms,vsj->mvj", col_hot.astype(jnp.bfloat16), far_blocks, preferred_element_type=jnp.float32
    ).astype(jnp.bfloat16)
    picked_near = jnp.einsum(
        "ms,vsj->mvj", row_hot.astype(jnp.bfloat16), near_blocks, preferred_element_type=jnp.float32
    ).astype(jnp.bfloat16)
    forward = jnp.einsum("mij,mvj->mvi", matrices, picked_far, preferred_element_type=jnp.float32)
    backward = jnp.einsum("mij,mvi->mvj", matrices, picked_near, preferred_element_type=jnp.float32)
    direct = jnp.einsum(
        "ms,mvi->vsi",
        (row_hot & active[:, None]).astype(jnp.float32),
        forward,
        precision=lax.Precision.HIGHEST,
    )
    mirrored = jnp.einsum(
        "ms,mvj->vsj",
        (col_hot & mirror[:, None]).astype(jnp.float32),
        backward,
        precision=lax.Precision.HIGHEST,
    )
    mirrored = mirrored.reshape(nvec, seg_len)
    direct = direct.reshape(nvec, seg_len)
    for step_bit in range(levels):
        arrived = from_behind(mirrored, "row", 1 << step_bit)
        mirrored = jnp.where((col_place >> step_bit) % 2 == 1, arrived, mirrored)
    base = direct + mirrored
    return lax.psum_scatter(base, "col", scatter_dimension=1, tiled=True)


def solution(mesh):
    return jax.shard_map(
        per_device,
        mesh=mesh,
        in_specs=(
            P(None, ("row", "col")),
            P("row", "col"),
            P("row", "col", None, None),
            P("row", "col", None, None, None),
        ),
        out_specs=P(None, ("row", "col")),
        check_vma=False,
    )
```

profile of v0, /device:TPU:1, one launch (start us, length us, event | category | flops | bytes accessed | tf_op | source)
XLA Modules:
  0.0 236.7 jit_solution(16063728289879375630)
XLA Ops:
  6.5 0.0 copy-start
  6.5 0.0 reduce-scatter.2.cloned.1.call-start
  6.5 53.1 %all_gather.3 = bf16[8,8192]{1,0:T(8,128)(2,1)S(1)} all-gather(bf16[8,512]{1,0:T(8,128)(2,1)} %param.4), channel_id=1, replica_groups=mesh['row'=32,'col'=16] {'col'}, dimensions={1}, use_global_device_ids=true | all-gather | bytes 139264 | tf_op jit(solution)/shard_map/all_gather | solution.py:16
  59.6 9.8 %collective-permute-start = (bf16[8,8192]{1,0:T(8,128)(2,1)S(1)}, bf16[8,8192]{1,0:T(8,128)(2,1)S(1)}, u32[]{:S(2)}, u32[]{:S(2)}) collective-permute-start(bf16[8,8192]{1,0:T(8,128)(2,1)S(1)} %all_gather.3), channel_id=1, source_target_pairs={{0,496},{16,0},{32,16},{48,32},{64,48},{80,64},{96,80},{112,96},{1... | collective-permute-start | bytes 393224 | tf_op jit(solution)/shard_map/ppermute | solution.py:10
  70.1 0.8 slice_bitcast_fusion
  70.8 0.2 fusion.6
  71.1 0.0 copy-done
  71.1 0.6 fusion
  71.7 1.4 collective-permute-done
  73.2 6.1 %collective-permute-start.1 = (bf16[8,8192]{1,0:T(8,128)(2,1)S(1)}, bf16[8,8192]{1,0:T(8,128)(2,1)S(1)}, u32[]{:S(2)}, u32[]{:S(2)}) collective-permute-start(bf16[8,8192]{1,0:T(8,128)(2,1)S(1)} %broadcast_select_fusion.1), channel_id=1, source_target_pairs={{0,480},{16,496},{32,0},{48,16},{64,32},{80,48},{96,64},{112,80},{... | collective-permute-start | bytes 393224 | tf_op jit(solution)/shard_map/ppermute | solution.py:10
  79.2 0.3 convolution_bitcast_fusion
  79.5 0.2 copy.29
  79.7 1.9 collective-permute-start.4
  81.7 0.0 collective-permute-done.1
  81.7 4.2 %collective-permute-start.2 = (bf16[8,8192]{1,0:T(8,128)(2,1)S(1)}, bf16[8,8192]{1,0:T(8,128)(2,1)S(1)}, u32[]{:S(2)}, u32[]{:S(2)}) collective-permute-start(bf16[8,8192]{1,0:T(8,128)(2,1)S(1)} %broadcast_select_fusion.3), channel_id=1, source_target_pairs={{0,448},{16,464},{32,480},{48,496},{64,0},{80,16},{96,32},{112,48}... | collective-permute-start | bytes 393224 | tf_op jit(solution)/shard_map/ppermute | solution.py:10
  85.9 0.0 collective-permute-done.4
  85.9 0.2 broadcast_select_fusion
  86.1 5.8 %collective-permute-start.5 = (f32[8,8192]{1,0:T(8,128)S(1)}, f32[8,8192]{1,0:T(8,128)S(1)}, u32[]{:S(2)}, u32[]{:S(2)}) collective-permute-start(f32[8,8192]{1,0:T(8,128)S(1)} %broadcast_select_fusion), channel_id=1, source_target_pairs={{0,32},{16,48},{32,64},{48,80},{64,96},{80,112},{96,128},{112,144}... | collective-permute-start | bytes 786440 | tf_op jit(solution)/shard_map/ppermute | solution.py:10
  91.9 0.0 collective-permute-done.2
  91.9 1.9 collective-permute-start.3
  93.9 3.2 %collective-permute-done.5 = f32[8,8192]{1,0:T(8,128)S(1)} collective-permute-done((f32[8,8192]{1,0:T(8,128)S(1)}, f32[8,8192]{1,0:T(8,128)S(1)}, u32[]{:S(2)}, u32[]{:S(2)}) %collective-permute-start.5) | collective-permute-done | bytes 262176 | tf_op jit(solution)/shard_map/ppermute | solution.py:10
  97.1 5.3 %collective-permute-start.6 = (f32[8,8192]{1,0:T(8,128)S(1)}, f32[8,8192]{1,0:T(8,128)S(1)}, u32[]{:S(2)}, u32[]{:S(2)}) collective-permute-start(f32[8,8192]{1,0:T(8,128)S(1)} %broadcast_select_fusion.2), channel_id=1, source_target_pairs={{0,64},{16,80},{32,96},{48,112},{64,128},{80,144},{96,160},{112,17... | collective-permute-start | bytes 786440 | tf_op jit(solution)/shard_map/ppermute | solution.py:10
  102.4 0.0 collective-permute-done.3
  102.4 0.2 fusion.8
  102.7 5.8 %collective-permute-done.6 = f32[8,8192]{1,0:T(8,128)S(1)} collective-permute-done((f32[8,8192]{1,0:T(8,128)S(1)}, f32[8,8192]{1,0:T(8,128)S(1)}, u32[]{:S(2)}, u32[]{:S(2)}) %collective-permute-start.6) | collective-permute-done | bytes 262176 | tf_op jit(solution)/shard_map/ppermute | solution.py:10
  108.5 2.3 collective-permute-start.7
  110.8 1.2 fusion.2
  112.0 0.3 convolution_bitcast_fusion.1
  112.3 5.4 %collective-permute-done.7 = f32[8,8192]{1,0:T(8,128)S(1)} collective-permute-done((f32[8,8192]{1,0:T(8,128)S(1)}, f32[8,8192]{1,0:T(8,128)S(1)}, u32[]{:S(2)}, u32[]{:S(2)}) %collective-permute-start.7) | collective-permute-done | bytes 262176 | tf_op jit(solution)/shard_map/ppermute | solution.py:10
  117.7 0.9 bitcast_add_fusion
  118.6 0.0 reduce-scatter.2.cloned.1.call-update
  118.6 111.3 %reduce-scatter.2.cloned.1.call-done = f32[8,512]{1,0:T(8,128)} async-done(((f32[8,8192]{1,0:T(8,128)}), f32[8,512]{1,0:T(8,128)}) %reduce-scatter.2.cloned.1.call-update) | async-done | bytes 16400 | tf_op jit(solution)/shard_map/reduce_scatter | solution.py:62
  (10 shorter events, 0.1 us)
Async XLA Ops:
  6.5 64.5 %copy-start = (bf16[1,1,64,128,128]{4,3,2,1,0:T(8,128)(2,1)S(1)}, bf16[1,1,64,128,128]{4,3,2,1,0:T(8,128)(2,1)}, u32[]{:S(2)}) copy-start(bf16[1,1,64,128,128]{4,3,2,1,0:T(8,128)(2,1)} %param.7) | copy-start | bytes 6291460
  6.5 65.2 %copy-start.1 = (s32[1,1,2,64]{3,2,1,0:T(2,128)S(1)}, s32[1,1,2,64]{3,2,1,0:T(2,128)}, u32[]{:S(2)}) copy-start(s32[1,1,2,64]{3,2,1,0:T(2,128)} %param.6) | copy-start | bytes 1540
  6.5 223.3 %reduce-scatter.2.cloned.1.call-start = ((), (), s32[]{:S(2)}) async-start(), calls=%async_computation.1 | async-start | bytes 278528 | tf_op jit(solution)/shard_map/reduce_scatter | solution.py:62
  59.6 13.5 %collective-permute-start = (bf16[8,8192]{1,0:T(8,128)(2,1)S(1)}, bf16[8,8192]{1,0:T(8,128)(2,1)S(1)}, u32[]{:S(2)}, u32[]{:S(2)}) collective-permute-start(bf16[8,8192]{1,0:T(8,128)(2,1)S(1)} %all_gather.3), channel_id=1, source_target_pairs={{0,496},{16,0},{32,16},{48,32},{64,48},{80,64},{96,80},{112,96},{1... | collective-permute-start | bytes 393224 | tf_op jit(solution)/shard_map/ppermute | solution.py:10
  73.2 8.5 %collective-permute-start.1 = (bf16[8,8192]{1,0:T(8,128)(2,1)S(1)}, bf16[8,8192]{1,0:T(8,128)(2,1)S(1)}, u32[]{:S(2)}, u32[]{:S(2)}) collective-permute-start(bf16[8,8192]{1,0:T(8,128)(2,1)S(1)} %broadcast_select_fusion.1), channel_id=1, source_target_pairs={{0,480},{16,496},{32,0},{48,16},{64,32},{80,48},{96,64},{112,80},{... | collective-permute-start | bytes 393224 | tf_op jit(solution)/shard_map/ppermute | solution.py:10
  79.7 6.2 %collective-permute-start.4 = (f32[8,8192]{1,0:T(8,128)S(1)}, f32[8,8192]{1,0:T(8,128)S(1)}, u32[]{:S(2)}, u32[]{:S(2)}) collective-permute-start(f32[8,8192]{1,0:T(8,128)S(1)} %bitcast.45), channel_id=1, source_target_pairs={{0,16},{16,32},{32,48},{48,64},{64,80},{80,96},{96,112},{112,128},... | collective-permute-start | bytes 786440 | tf_op jit(solution)/shard_map/ppermute | solution.py:10
  81.7 10.2 %collective-permute-start.2 = (bf16[8,8192]{1,0:T(8,128)(2,1)S(1)}, bf16[8,8192]{1,0:T(8,128)(2,1)S(1)}, u32[]{:S(2)}, u32[]{:S(2)}) collective-permute-start(bf16[8,8192]{1,0:T(8,128)(2,1)S(1)} %broadcast_select_fusion.3), channel_id=1, source_target_pairs={{0,448},{16,464},{32,480},{48,496},{64,0},{80,16},{96,32},{112,48}... | collective-permute-start | bytes 393224 | tf_op jit(solution)/shard_map/ppermute | solution.py:10
  86.1 11.0 %collective-permute-start.5 = (f32[8,8192]{1,0:T(8,128)S(1)}, f32[8,8192]{1,0:T(8,128)S(1)}, u32[]{:S(2)}, u32[]{:S(2)}) collective-permute-start(f32[8,8192]{1,0:T(8,128)S(1)} %broadcast_select_fusion), channel_id=1, source_target_pairs={{0,32},{16,48},{32,64},{48,80},{64,96},{80,112},{96,128},{112,144}... | collective-permute-start | bytes 786440 | tf_op jit(solution)/shard_map/ppermute | solution.py:10
  91.9 10.5 %collective-permute-start.3 = (bf16[8,8192]{1,0:T(8,128)(2,1)S(1)}, bf16[8,8192]{1,0:T(8,128)(2,1)S(1)}, u32[]{:S(2)}, u32[]{:S(2)}) collective-permute-start(bf16[8,8192]{1,0:T(8,128)(2,1)S(1)} %broadcast_select_fusion.5), channel_id=1, source_target_pairs={{0,384},{16,400},{32,416},{48,432},{64,448},{80,464},{96,480},{112... | collective-permute-start | bytes 393224 | tf_op jit(solution)/shard_map/ppermute | solution.py:10
  97.1 11.3 %collective-permute-start.6 = (f32[8,8192]{1,0:T(8,128)S(1)}, f32[8,8192]{1,0:T(8,128)S(1)}, u32[]{:S(2)}, u32[]{:S(2)}) collective-permute-start(f32[8,8192]{1,0:T(8,128)S(1)} %broadcast_select_fusion.2), channel_id=1, source_target_pairs={{0,64},{16,80},{32,96},{48,112},{64,128},{80,144},{96,160},{112,17... | collective-permute-start | bytes 786440 | tf_op jit(solution)/shard_map/ppermute | solution.py:10
  108.5 9.2 %collective-permute-start.7 = (f32[8,8192]{1,0:T(8,128)S(1)}, f32[8,8192]{1,0:T(8,128)S(1)}, u32[]{:S(2)}, u32[]{:S(2)}) collective-permute-start(f32[8,8192]{1,0:T(8,128)S(1)} %broadcast_select_fusion.4), channel_id=1, source_target_pairs={{0,128},{16,144},{32,160},{48,176},{64,192},{80,208},{96,224},{112... | collective-permute-start | bytes 786440 | tf_op jit(solution)/shard_map/ppermute | solution.py:10
Sparse Core Ops, SparseCore 0:
  118.7 111.0 reduce-scatter.1
where the time goes:
time: 238 us; the launch traced here: 237 us
  waiting for transfers between devices  127 us (53%)
  blocking collectives  53.1 us (22%)
  starting transfers between devices  37.3 us (16%)
  between operations  14.3 us (6%)
  matrix products  2.86 us (1%)
    reduce_scatter x1, waiting for transfers between devices, per_device(): return lax.psum_scatter(base, 'col', scatter_dimension=1, tiled=True)  111 us
    all_gather x1, blocking collectives, per_device(): home_seg = lax.all_gather(vectors, 'col', axis=1, tiled=True)  53.1 us
    ppermute x8, starting transfers between devices, from_behind(): return lax.ppermute(value, axis, pairs)  37.3 us
    ppermute x8, waiting for transfers between devices, from_behind(): return lax.ppermute(value, axis, pairs)  15.8 us
  transfers between devices with their start and end apart: 9, of which 5 were waited for; matrix products, arithmetic and copies ran while one was open for 2% of the time, Pallas kernels for 0%

commit v1 on v0

v1 whole, which is shorter than its diff:
```python
import jax
import jax.numpy as jnp
from jax import lax
from jax.experimental import pallas as pl
from jax.experimental.pallas import tpu as pltpu
from jax.sharding import PartitionSpec as P

PLACES = ("row", "col")


def joint_pairs(to_second):
    rows = lax.axis_size("row")
    cols = lax.axis_size("col")
    pairs = []
    for r in range(rows):
        for c in range(cols):
            first, second = r * cols + c, ((r + c) % rows) * cols + c
            pairs.append((first, second) if to_second else (second, first))
    return pairs


def mirrored_kernel(count_ref, index_ref, near_ref, blocks_ref, out_ref):
    off_first = lax.axis_index("col") != 0
    out_ref[...] = jnp.zeros_like(out_ref)
    live = count_ref[0, 0]
    for m in range(blocks_ref.shape[2]):
        first = index_ref[0, 0, 0, m]
        second = index_ref[0, 0, 1, m]
        keep = (m < live) & (off_first | (first != second))
        product = lax.dot_general(
            near_ref[first], blocks_ref[0, 0, m], (((1,), (0,)), ((), ())), preferred_element_type=jnp.float32
        )
        out_ref[second] = out_ref[second] + jnp.where(keep, product, 0.0)


def direct_kernel(count_ref, index_ref, far_ref, blocks_ref, out_ref):
    out_ref[...] = jnp.zeros_like(out_ref)
    live = count_ref[0, 0]
    for m in range(blocks_ref.shape[2]):
        first = index_ref[0, 0, 0, m]
        second = index_ref[0, 0, 1, m]
        product = lax.dot_general(
            far_ref[second], blocks_ref[0, 0, m], (((1,), (1,)), ((), ())), preferred_element_type=jnp.float32
        )
        out_ref[first] = out_ref[first] + jnp.where(m < live, product, 0.0)


def apply_slots(kernel, count, index, segment, blocks):
    smem = pl.BlockSpec(memory_space=pltpu.SMEM)
    vmem = pl.BlockSpec(memory_space=pltpu.VMEM)
    flops = 2 * segment.shape[1] * blocks.size
    return pl.pallas_call(
        kernel,
        out_shape=jax.ShapeDtypeStruct(segment.shape, jnp.float32),
        in_specs=[smem, smem, vmem, vmem],
        out_specs=vmem,
        compiler_params=pltpu.CompilerParams(vmem_limit_bytes=16 * 1024 * 1024),
        cost_estimate=pl.CostEstimate(flops=flops, bytes_accessed=2 * blocks.size, transcendentals=0),
    )(count, index, segment, blocks)


def per_device(vectors, block_count, block_index, blocks):
    cols = lax.axis_size("col")
    size = blocks.shape[-1]
    nvec, width = vectors.shape
    own = vectors.reshape(nvec, width // size, size).transpose(1, 0, 2)
    near = lax.all_to_all(jnp.tile(own, (cols, 1, 1)), "col", 0, 0, tiled=True)
    far = lax.ppermute(near, PLACES, joint_pairs(False))
    mirrored = apply_slots(mirrored_kernel, block_count, block_index, near, blocks)
    arrived = lax.ppermute(mirrored, PLACES, joint_pairs(True))
    direct = apply_slots(direct_kernel, block_count, block_index, far, blocks)
    shares = lax.all_to_all(direct + arrived, "col", 0, 0, tiled=True)
    total = shares.reshape(cols, width // size, nvec, size).sum(0)
    return total.transpose(1, 0, 2).reshape(nvec, width)


def solution(mesh):
    return jax.shard_map(
        per_device,
        mesh=mesh,
        in_specs=(
            P(None, ("row", "col")),
            P("row", "col"),
            P("row", "col", None, None),
            P("row", "col", None, None, None),
        ),
        out_specs=P(None, ("row", "col")),
        check_vma=False,
    )
```

time: 238 us -> 87.4 us (0.37)
  the two profiles are of different devices: /device:TPU:1 before, /device:TPU:34 now
where the time goes in v1:
time: 87.4 us; the launch traced here: 87.1 us
  blocking collectives  43.5 us (50%)
  starting transfers between devices  18.3 us (21%)
  waiting for transfers between devices  17.3 us (20%)
  local copies, waits for them, and re-layouts  3.64 us (4%)
  Pallas kernels  2.95 us (3%)
    all_to_all x1, blocking collectives, per_device(): shares = lax.all_to_all(direct + arrived, 'col', 0, 0, tiled=True)  43.5 us
    all_to_all x1, waiting for transfers between devices, per_device(): near = lax.all_to_all(jnp.tile(own, (cols, 1, 1)), 'col', 0, 0, tiled=True)  17.3 us
    all_to_all x1, starting transfers between devices, per_device(): near = lax.all_to_all(jnp.tile(own, (cols, 1, 1)), 'col', 0, 0, tiled=True)  16.9 us
    pallas_call x2, Pallas kernels, apply_slots(): pl.pallas_call(kernel, out_shape=jax.ShapeDtypeStruct(segment.shape, jnp....  2.95 us
    unnamed x6, local copies, waits for them, and re-layouts  2.27 us
  transfers between devices with their start and end apart: 3, of which 1 were waited for; matrix products, arithmetic and copies ran while one was open for 0% of the time, Pallas kernels for 2%

profile of v1, /device:TPU:34, one launch (start us, length us, event | category | flops | bytes accessed | tf_op | source)
XLA Modules:
  0.0 87.1 jit_solution(1630999973420878725)
XLA Ops:
  0.0 1.4 %tile.4 = bf16[16,4,8,128]{3,2,1,0:T(8,128)(2,1)} broadcast(bf16[4,8,128]{2,1,0:T(8,128)(2,1)} %bitcast.9), dimensions={1,2,3} | broadcast | bytes 139264 | tf_op jit(solution)/shard_map/tile | solution.py:67
  1.4 16.9 %all-to-all-start = ((bf16[64,8,128]{2,1,0:T(8,128)(2,1)}), bf16[64,8,128]{2,1,0:T(8,128)(2,1)S(1)}, u32[]{:S(2)}, u32[]{:S(2)}) async-start(bf16[64,8,128]{2,1,0:T(8,128)(2,1)} %bitcast.2), calls=%async_computation | async-start | bytes 262144 | tf_op jit(solution)/shard_map/all_to_all | solution.py:67
  18.9 17.3 %all-to-all-done.near_ref = bf16[64,8,128]{2,1,0:T(8,128)(2,1)S(1)} async-done(((bf16[64,8,128]{2,1,0:T(8,128)(2,1)}), bf16[64,8,128]{2,1,0:T(8,128)(2,1)S(1)}, u32[]{:S(2)}, u32[]{:S(2)}) %all-to-all-start) | async-done | bytes 131104 | tf_op jit(solution)/shard_map/all_to_all | solution.py:67
  36.3 0.0 copy-start
  36.3 1.6 %copy-done = bf16[1,1,64,128,128]{4,3,2,1,0:T(8,128)(2,1)S(1)} copy-done((bf16[1,1,64,128,128]{4,3,2,1,0:T(8,128)(2,1)S(1)}, bf16[1,1,64,128,128]{4,3,2,1,0:T(8,128)(2,1)}, u32[]{:S(2)}) %copy-start) | copy-done | bytes 2097176
  37.9 0.0 copy-start.2
  37.9 0.7 copy-done.2
  38.5 0.0 copy-start.1
  38.5 1.2 %shard_map.47 = f32[64,8,128]{2,1,0:T(8,128)S(1)} custom-call(s32[1,1]{1,0:T(1,128)S(6)} %copy.5.count_ref, s32[1,1,2,64]{3,2,1,0:T(2,128)S(1)} %copy-done.2, bf16[64,8,128]{2,1,0:T(8,128)(2,1)S(1)} %all-to-all-done.near_ref, bf16[1,1,64,128,128]{4,3,2,1,0:T(8,128)(2,1)S(1)} %copy-done), custom_call_target="tpu_custom_call" | custom-call | flops 16777216 | bytes 2097152 | tf_op jit(solution)/shard_map/pallas_call | solution.py:52
  39.7 0.7 collective-permute-start.1
  40.4 0.7 collective-permute-start
  41.1 0.0 collective-permute-done.far_ref
  41.1 0.0 copy-done.1
  41.1 1.7 %shard_map.46 = f32[64,8,128]{2,1,0:T(8,128)S(1)} custom-call(s32[1,1]{1,0:T(1,128)S(6)} %copy.5.count_ref, s32[1,1,2,64]{3,2,1,0:T(2,128)S(1)} %copy-done.2, bf16[64,8,128]{2,1,0:T(8,128)(2,1)S(1)} %collective-permute-done.far_ref, bf16[1,1,64,128,128]{4,3,2,1,0:T(8,128)(2,1)S(1)} %copy-done.1), custom_call_target="tpu_custom_call" | custom-call | flops 16777216 | bytes 2097152 | tf_op jit(solution)/shard_map/pallas_call | solution.py:52
  42.9 0.0 collective-permute-done.1
  42.9 43.5 %all_to_all.10 = f32[64,8,128]{2,1,0:T(8,128)S(1)} all-to-all(f32[64,8,128]{2,1,0:T(8,128)S(1)} %add.3), channel_id=1, replica_groups=mesh['row'=32,'col'=16] {'col'}, dimensions={0} | all-to-all | bytes 524288 | tf_op jit(solution)/shard_map/all_to_all | solution.py:72
  86.4 0.6 reduce_sum.9
  (1 shorter events, 0.0 us)
Async XLA Ops:
  1.4 34.9 %all-to-all-start = ((bf16[64,8,128]{2,1,0:T(8,128)(2,1)}), bf16[64,8,128]{2,1,0:T(8,128)(2,1)S(1)}, u32[]{:S(2)}, u32[]{:S(2)}) async-start(bf16[64,8,128]{2,1,0:T(8,128)(2,1)} %bitcast.2), calls=%async_computation | async-start | bytes 262144 | tf_op jit(solution)/shard_map/all_to_all | solution.py:67
  36.3 1.6 %copy-start = (bf16[1,1,64,128,128]{4,3,2,1,0:T(8,128)(2,1)S(1)}, bf16[1,1,64,128,128]{4,3,2,1,0:T(8,128)(2,1)}, u32[]{:S(2)}) copy-start(bf16[1,1,64,128,128]{4,3,2,1,0:T(8,128)(2,1)} %blocks_ref.3) | copy-start | bytes 6291460
  37.9 0.7 copy-start.2
  38.5 2.6 %copy-start.1 = (bf16[1,1,64,128,128]{4,3,2,1,0:T(8,128)(2,1)S(1)}, bf16[1,1,64,128,128]{4,3,2,1,0:T(8,128)(2,1)}, u32[]{:S(2)}) copy-start(bf16[1,1,64,128,128]{4,3,2,1,0:T(8,128)(2,1)} %blocks_ref.3) | copy-start | bytes 6291460
  39.7 3.1 %collective-permute-start.1 = (f32[64,8,128]{2,1,0:T(8,128)S(1)}, f32[64,8,128]{2,1,0:T(8,128)S(1)}, u32[]{:S(2)}, u32[]{:S(2)}) collective-permute-start(f32[64,8,128]{2,1,0:T(8,128)S(1)} %shard_map.47), channel_id=1, source_target_pairs={{0,0},{1,17},{2,34},{3,51},{4,68},{5,85},{6,102},{7,119},{8,136},{... | collective-permute-start | bytes 786440 | tf_op jit(solution)/shard_map/ppermute | solution.py:70
  40.4 0.7 collective-permute-start

commit v2 on v1

v2 whole, which is shorter than its diff:
```python
import functools

import jax
import jax.numpy as jnp
from jax import lax
from jax.experimental import pallas as pl
from jax.experimental.pallas import tpu as pltpu
from jax.sharding import PartitionSpec as P

PLACES = ("row", "col")
TOP = 32767.0
STEPS = 16.0
LEAST = 1e-33


def joint_pairs(to_second):
    rows = lax.axis_size("row")
    cols = lax.axis_size("col")
    pairs = []
    for r in range(rows):
        for c in range(cols):
            first, second = r * cols + c, ((r + c) % rows) * cols + c
            pairs.append((first, second) if to_second else (second, first))
    return pairs


def encode(values, out_ref, chunk):
    peak = functools.reduce(jnp.maximum, [jnp.abs(v) for v in values])
    peak = jnp.maximum(jnp.max(peak, axis=-1, keepdims=True), LEAST)
    power = jnp.ceil(jnp.log2(peak / TOP) * STEPS)
    power = jnp.broadcast_to(power, values[0].shape)
    up = jnp.exp2(power * (-1.0 / STEPS))
    for b, v in enumerate(values):
        code = jnp.clip(jnp.round(v * up), -TOP, TOP)
        out_ref[chunk, b] = code.astype(jnp.int32).astype(jnp.int16)
    out_ref[chunk, len(values)] = power.astype(jnp.int32).astype(jnp.int16)


def decode(in_ref, chunk):
    last = in_ref.shape[1] - 1

    def number(b):
        return in_ref[chunk, b].astype(jnp.int32).astype(jnp.float32)

    down = jnp.exp2(number(last) * (1.0 / STEPS))
    return [number(b) * down for b in range(last)]


def spread_kernel(own_ref, out_ref):
    for n in range(out_ref.shape[0]):
        out_ref[n] = own_ref[...]


def mirrored_kernel(count_ref, index_ref, near_ref, blocks_ref, out_ref, sum_ref):
    off_first = lax.axis_index("col") != 0
    sum_ref[...] = jnp.zeros_like(sum_ref)
    live = count_ref[0, 0]
    for m in range(blocks_ref.shape[2]):
        first = index_ref[0, 0, 0, m]
        second = index_ref[0, 0, 1, m]
        keep = (m < live) & (off_first | (first != second))
        product = lax.dot_general(
            near_ref[first], blocks_ref[0, 0, m], (((1,), (0,)), ((), ())), preferred_element_type=jnp.float32
        )
        sum_ref[second] = sum_ref[second] + jnp.where(keep, product, 0.0)
    chunks, each = out_ref.shape[0], out_ref.shape[1] - 1
    for n in range(chunks):
        encode([sum_ref[n * each + b] for b in range(each)], out_ref, n)


def direct_kernel(count_ref, index_ref, far_ref, blocks_ref, out_ref):
    out_ref[...] = jnp.zeros_like(out_ref)
    live = count_ref[0, 0]
    for m in range(blocks_ref.shape[2]):
        first = index_ref[0, 0, 0, m]
        second = index_ref[0, 0, 1, m]
        product = lax.dot_general(
            far_ref[second], blocks_ref[0, 0, m], (((1,), (1,)), ((), ())), preferred_element_type=jnp.float32
        )
        out_ref[first] = out_ref[first] + jnp.where(m < live, product, 0.0)


def join_kernel(direct_ref, arrived_ref, out_ref):
    chunks, each = out_ref.shape[0], out_ref.shape[1] - 1
    for n in range(chunks):
        arrived = decode(arrived_ref, n)
        encode([direct_ref[n * each + b] + arrived[b] for b in range(each)], out_ref, n)


def total_kernel(shares_ref, out_ref):
    chunks = shares_ref.shape[0]
    total = decode(shares_ref, 0)
    for n in range(1, chunks):
        total = [a + b for a, b in zip(total, decode(shares_ref, n))]
    for b, value in enumerate(total):
        out_ref[b] = value


def call(kernel, out_shape, dtype, args, flops, scalars=0, scratch=()):
    smem = pl.BlockSpec(memory_space=pltpu.SMEM)
    vmem = pl.BlockSpec(memory_space=pltpu.VMEM)
    return pl.pallas_call(
        kernel,
        out_shape=jax.ShapeDtypeStruct(out_shape, dtype),
        in_specs=[smem] * scalars + [vmem] * (len(args) - scalars),
        out_specs=vmem,
        scratch_shapes=scratch,
        compiler_params=pltpu.CompilerParams(vmem_limit_bytes=16 * 1024 * 1024),
        cost_estimate=pl.CostEstimate(flops=flops, bytes_accessed=1 << 20, transcendentals=0),
    )(*args)


def per_device(vectors, block_count, block_index, blocks):
    cols = lax.axis_size("col")
    size = blocks.shape[-1]
    nvec, width = vectors.shape
    each = width // size
    work = 2 * nvec * blocks.size
    own = vectors.reshape(nvec, each, size).transpose(1, 0, 2)
    copies = call(spread_kernel, (cols,) + own.shape, own.dtype, (own,), 1000 * work)
    near = lax.all_to_all(copies.reshape(cols * each, nvec, size), "col", 0, 0, tiled=True)
    far = lax.ppermute(near, PLACES, joint_pairs(False))
    coded = (cols, each + 1, nvec, size)
    sums = pltpu.VMEM(near.shape, jnp.float32)
    mirrored = call(mirrored_kernel, coded, jnp.int16, (block_count, block_index, near, blocks), work, 2, [sums])
    arrived = lax.ppermute(mirrored, PLACES, joint_pairs(True))
    direct = call(direct_kernel, near.shape, jnp.float32, (block_count, block_index, far, blocks), 1000 * work, 2)
    shares = call(join_kernel, coded, jnp.int16, (direct, arrived), work)
    shares = lax.all_to_all(shares, "col", 0, 0, tiled=True)
    total = call(total_kernel, own.shape, jnp.float32, (shares,), work)
    return total.transpose(1, 0, 2).reshape(nvec, width)


def solution(mesh):
    return jax.shard_map(
        per_device,
        mesh=mesh,
        in_specs=(
            P(None, ("row", "col")),
            P("row", "col"),
            P("row", "col", None, None),
            P("row", "col", None, None, None),
        ),
        out_specs=P(None, ("row", "col")),
        check_vma=False,
    )
```

time: 87.4 us -> 76 us (0.87)
  the two profiles are of different devices: /device:TPU:34 before, /device:TPU:1 now
where the time goes in v2:
time: 76 us; the launch traced here: 75.2 us
  blocking collectives  68.5 us (90%)
  Pallas kernels  3.96 us (5%)
  starting transfers between devices  1.33 us (2%)
    all_to_all x1, blocking collectives, per_device(): shares = lax.all_to_all(shares, 'col', 0, 0, tiled=True)  36 us
    all_to_all x1, blocking collectives, per_device(): lax.all_to_all(copies.reshape(cols * each, nvec, size), 'col', 0, 0, tile...  32.4 us
    pallas_call x5, Pallas kernels, call(): pl.pallas_call(kernel, out_shape=jax.ShapeDtypeStruct(out_shape, dtype),...  3.96 us
  transfers between devices with their start and end apart: 2, of which 0 were waited for; matrix products, arithmetic and copies ran while one was open for 0% of the time, Pallas kernels for 4%

profile of v2, /device:TPU:1, one launch (start us, length us, event | category | flops | bytes accessed | tf_op | source)
XLA Modules:
  0.0 75.2 jit_solution(5092684490941691921)
XLA Ops:
  0.0 0.0 copy-start.2
  0.0 0.7 copy-done.2
  0.7 0.0 copy-start
  0.7 0.0 copy-start.1
  0.7 32.4 %all_to_all.10.near_ref = bf16[64,8,128]{2,1,0:T(8,128)(2,1)S(1)} all-to-all(bf16[64,8,128]{2,1,0:T(8,128)(2,1)S(1)} %bitcast.7), channel_id=1, replica_groups=mesh['row'=32,'col'=16] {'col'}, dimensions={0} | all-to-all | bytes 262144 | tf_op jit(solution)/shard_map/all_to_all | solution.py:121
  33.1 0.7 collective-permute-start
  34.5 0.0 copy-done
  34.5 0.0 copy-done.1
  34.5 1.4 %shard_map.48 = s16[16,5,8,128]{3,2,1,0:T(8,128)(2,1)S(1)} custom-call(s32[1,1]{1,0:T(1,128)S(6)} %copy.5.count_ref, s32[1,1,2,64]{3,2,1,0:T(2,128)S(1)} %copy-done.1, bf16[64,8,128]{2,1,0:T(8,128)(2,1)S(1)} %all_to_all.10.near_ref, bf16[1,1,64,128,128]{4,3,2,1,0:T(8,128)(2,1)S(1)} %copy-done), custom_call_target="tpu_custom_call" | custom-call | flops 16777216 | bytes 1048576 | tf_op jit(solution)/shard_map/pallas_call | solution.py:102
  35.9 0.7 collective-permute-start.1
  36.5 0.0 collective-permute-done.far_ref
  36.5 1.7 %shard_map.47.direct_ref = f32[64,8,128]{2,1,0:T(8,128)S(1)} custom-call(s32[1,1]{1,0:T(1,128)S(6)} %copy.5.count_ref, s32[1,1,2,64]{3,2,1,0:T(2,128)S(1)} %copy-done.1, bf16[64,8,128]{2,1,0:T(8,128)(2,1)S(1)} %collective-permute-done.far_ref, bf16[1,1,64,128,128]{4,3,2,1,0:T(8,128)(2,1)S(1)} %copy-done), custom_call_target="tpu_custom_call" | custom-call | flops 16777216000 | bytes 1048576 | tf_op jit(solution)/shard_map/pallas_call | solution.py:102
  38.3 0.0 collective-permute-done.1.arrived_ref
  38.3 0.2 shard_map.49
  38.5 36.0 %all_to_all.11.shares_ref = s16[16,5,8,128]{3,2,1,0:T(8,128)(2,1)S(1)} all-to-all(s16[16,5,8,128]{3,2,1,0:T(8,128)(2,1)S(1)} %shard_map.49), channel_id=1, replica_groups=mesh['row'=32,'col'=16] {'col'}, dimensions={0} | all-to-all | bytes 327680 | tf_op jit(solution)/shard_map/all_to_all | solution.py:129
  74.5 0.7 shard_map.50
  (1 shorter events, 0.0 us)
Async XLA Ops:
  0.0 0.7 copy-start.2
  0.7 33.8 %copy-start = (bf16[1,1,64,128,128]{4,3,2,1,0:T(8,128)(2,1)S(1)}, bf16[1,1,64,128,128]{4,3,2,1,0:T(8,128)(2,1)}, u32[]{:S(2)}) copy-start(bf16[1,1,64,128,128]{4,3,2,1,0:T(8,128)(2,1)} %blocks_ref.3) | copy-start | bytes 6291460
  0.7 33.8 %copy-start.1 = (s32[1,1,2,64]{3,2,1,0:T(2,128)S(1)}, s32[1,1,2,64]{3,2,1,0:T(2,128)}, u32[]{:S(2)}) copy-start(s32[1,1,2,64]{3,2,1,0:T(2,128)} %index_ref.3) | copy-start | bytes 1540
  33.1 3.4 %collective-permute-start = (bf16[64,8,128]{2,1,0:T(8,128)(2,1)S(1)}, bf16[64,8,128]{2,1,0:T(8,128)(2,1)S(1)}, u32[]{:S(2)}, u32[]{:S(2)}) collective-permute-start(bf16[64,8,128]{2,1,0:T(8,128)(2,1)S(1)} %all_to_all.10.near_ref), channel_id=1, source_target_pairs={{0,0},{17,1},{34,2},{51,3},{68,4},{85,5},{102,6},{119,7},{136,8},{... | collective-permute-start | bytes 393224 | tf_op jit(solution)/shard_map/ppermute | solution.py:122
  35.9 2.4 %collective-permute-start.1 = (s16[16,5,8,128]{3,2,1,0:T(8,128)(2,1)S(1)}, s16[16,5,8,128]{3,2,1,0:T(8,128)(2,1)S(1)}, u32[]{:S(2)}, u32[]{:S(2)}) collective-permute-start(s16[16,5,8,128]{3,2,1,0:T(8,128)(2,1)S(1)} %shard_map.48), channel_id=1, source_target_pairs={{0,0},{1,17},{2,34},{3,51},{4,68},{5,85},{6,102},{7,119},{8,136},{... | collective-permute-start | bytes 491528 | tf_op jit(solution)/shard_map/ppermute | solution.py:126

commit v3 on v2

--- a/solution.py
+++ b/solution.py
@@ -24,26 +24,24 @@
     return pairs
 
 
-def encode(values, out_ref, chunk):
+def encode(values):
     peak = functools.reduce(jnp.maximum, [jnp.abs(v) for v in values])
     peak = jnp.maximum(jnp.max(peak, axis=-1, keepdims=True), LEAST)
     power = jnp.ceil(jnp.log2(peak / TOP) * STEPS)
     power = jnp.broadcast_to(power, values[0].shape)
     up = jnp.exp2(power * (-1.0 / STEPS))
-    for b, v in enumerate(values):
-        code = jnp.clip(jnp.round(v * up), -TOP, TOP)
-        out_ref[chunk, b] = code.astype(jnp.int32).astype(jnp.int16)
-    out_ref[chunk, len(values)] = power.astype(jnp.int32).astype(jnp.int16)
+    codes = [jnp.clip(jnp.round(v * up), -TOP, TOP).astype(jnp.int32).astype(jnp.int16) for v in values]
+    return codes, power
+
+
+def number(code):
+    return code.astype(jnp.int32).astype(jnp.float32)
 
 
 def decode(in_ref, chunk):
     last = in_ref.shape[1] - 1
-
-    def number(b):
-        return in_ref[chunk, b].astype(jnp.int32).astype(jnp.float32)
-
-    down = jnp.exp2(number(last) * (1.0 / STEPS))
-    return [number(b) * down for b in range(last)]
+    down = jnp.exp2(number(in_ref[chunk, last]) * (1.0 / STEPS))
+    return [number(in_ref[chunk, b]) * down for b in range(last)]
 
 
 def spread_kernel(own_ref, out_ref):
@@ -51,7 +49,7 @@
         out_ref[n] = own_ref[...]
 
 
-def mirrored_kernel(count_ref, index_ref, near_ref, blocks_ref, out_ref, sum_ref):
+def mirrored_kernel(each, count_ref, index_ref, near_ref, blocks_ref, out_ref, sum_ref):
     off_first = lax.axis_index("col") != 0
     sum_ref[...] = jnp.zeros_like(sum_ref)
     live = count_ref[0, 0]
@@ -63,9 +61,15 @@
             near_ref[first], blocks_ref[0, 0, m], (((1,), (0,)), ((), ())), preferred_element_type=jnp.float32
         )
         sum_ref[second] = sum_ref[second] + jnp.where(keep, product, 0.0)
-    chunks, each = out_ref.shape[0], out_ref.shape[1] - 1
+    chunks = out_ref.shape[0] // each
+    lane = lax.broadcasted_iota(jnp.int32, out_ref.shape[1:], 1)
+    powers = jnp.zeros(out_ref.shape[1:], jnp.float32)
     for n in range(chunks):
-        encode([sum_ref[n * each + b] for b in range(each)], out_ref, n)
+        codes, power = encode([sum_ref[n * each + b] for b in range(each)])
+        powers = jnp.where(lane == n, power, powers)
+        for b, code in enumerate(codes):
+            out_ref[n * each + b] = code
+    out_ref[chunks * each] = powers.astype(jnp.int32).astype(jnp.int16)
 
 
 def direct_kernel(count_ref, index_ref, far_ref, blocks_ref, out_ref):
@@ -82,9 +86,14 @@
 
 def join_kernel(direct_ref, arrived_ref, out_ref):
     chunks, each = out_ref.shape[0], out_ref.shape[1] - 1
+    downs = jnp.exp2(number(arrived_ref[chunks * each]) * (1.0 / STEPS))
     for n in range(chunks):
-        arrived = decode(arrived_ref, n)
-        encode([direct_ref[n * each + b] + arrived[b] for b in range(each)], out_ref, n)
+        down = jnp.broadcast_to(downs[:, n : n + 1], downs.shape)
+        sums = [direct_ref[n * each + b] + number(arrived_ref[n * each + b]) * down for b in range(each)]
+        codes, power = encode(sums)
+        for b, code in enumerate(codes):
+            out_ref[n, b] = code
+        out_ref[n, each] = power.astype(jnp.int32).astype(jnp.int16)
 
 
 def total_kernel(shares_ref, out_ref):
@@ -122,7 +131,9 @@
     far = lax.ppermute(near, PLACES, joint_pairs(False))
     coded = (cols, each + 1, nvec, size)
     sums = pltpu.VMEM(near.shape, jnp.float32)
-    mirrored = call(mirrored_kernel, coded, jnp.int16, (block_count, block_index, near, blocks), work, 2, [sums])
+    lone = (cols * each + 1, nvec, size)
+    kernel = functools.partial(mirrored_kernel, each)
+    mirrored = call(kernel, lone, jnp.int16, (block_count, block_index, near, blocks), work, 2, [sums])
     arrived = lax.ppermute(mirrored, PLACES, joint_pairs(True))
     direct = call(direct_kernel, near.shape, jnp.float32, (block_count, block_index, far, blocks), 1000 * work, 2)
     shares = call(join_kernel, coded, jnp.int16, (direct, arrived), work)

time: 76 us -> 75.6 us (level)
  blocking collectives: 68.5 us -> 67.2 us
    all_to_all x1, blocking collectives: 36 us -> 34.8 us  [per_device(): shares = lax.all_to_all(shares, 'col', 0, 0, tiled=True)]
where the time goes in v3:
time: 75.6 us; the launch traced here: 74.3 us
  blocking collectives  67.2 us (89%)
  Pallas kernels  4.31 us (6%)
  starting transfers between devices  1.33 us (2%)
    all_to_all x1, blocking collectives, per_device(): shares = lax.all_to_all(shares, 'col', 0, 0, tiled=True)  34.8 us
    all_to_all x1, blocking collectives, per_device(): lax.all_to_all(copies.reshape(cols * each, nvec, size), 'col', 0, 0, tile...  32.4 us
    pallas_call x5, Pallas kernels, call(): pl.pallas_call(kernel, out_shape=jax.ShapeDtypeStruct(out_shape, dtype),...  4.31 us
  transfers between devices with their start and end apart: 2, of which 0 were waited for; matrix products, arithmetic and copies ran while one was open for 0% of the time, Pallas kernels for 4%

profile of v3, /device:TPU:1, one launch (start us, length us, event | category | flops | bytes accessed | tf_op | source)
XLA Modules:
  0.0 74.3 jit_solution(17437089315702525793)
XLA Ops:
  0.0 0.0 copy-start.2
  0.0 0.7 copy-done.2
  0.7 0.0 copy-start
  0.7 0.0 copy-start.1
  0.7 32.4 %all_to_all.10.near_ref = bf16[64,8,128]{2,1,0:T(8,128)(2,1)S(1)} all-to-all(bf16[64,8,128]{2,1,0:T(8,128)(2,1)S(1)} %bitcast.7), channel_id=1, replica_groups=mesh['row'=32,'col'=16] {'col'}, dimensions={0} | all-to-all | bytes 262144 | tf_op jit(solution)/shard_map/all_to_all | solution.py:130
  33.1 0.7 collective-permute-start
  34.5 0.0 copy-done
  34.5 0.0 copy-done.1
  34.5 1.4 %shard_map.48 = s16[65,8,128]{2,1,0:T(8,128)(2,1)S(1)} custom-call(s32[1,1]{1,0:T(1,128)S(6)} %copy.5.count_ref, s32[1,1,2,64]{3,2,1,0:T(2,128)S(1)} %copy-done.1, bf16[64,8,128]{2,1,0:T(8,128)(2,1)S(1)} %all_to_all.10.near_ref, bf16[1,1,64,128,128]{4,3,2,1,0:T(8,128)(2,1)S(1)} %copy-done), custom_call_target="tpu_custom_call" | custom-call | flops 16777216 | bytes 1048576 | tf_op jit(solution)/shard_map/pallas_call | solution.py:111
  35.9 0.7 collective-permute-start.1
  36.5 0.0 collective-permute-done.far_ref
  36.5 1.7 %shard_map.47.direct_ref = f32[64,8,128]{2,1,0:T(8,128)S(1)} custom-call(s32[1,1]{1,0:T(1,128)S(6)} %copy.5.count_ref, s32[1,1,2,64]{3,2,1,0:T(2,128)S(1)} %copy-done.1, bf16[64,8,128]{2,1,0:T(8,128)(2,1)S(1)} %collective-permute-done.far_ref, bf16[1,1,64,128,128]{4,3,2,1,0:T(8,128)(2,1)S(1)} %copy-done), custom_call_target="tpu_custom_call" | custom-call | flops 16777216000 | bytes 1048576 | tf_op jit(solution)/shard_map/pallas_call | solution.py:111
  38.3 0.0 collective-permute-done.1.arrived_ref
  38.3 0.5 shard_map.49
  38.8 34.8 %all_to_all.11.shares_ref = s16[16,5,8,128]{3,2,1,0:T(8,128)(2,1)S(1)} all-to-all(s16[16,5,8,128]{3,2,1,0:T(8,128)(2,1)S(1)} %shard_map.49), channel_id=1, replica_groups=mesh['row'=32,'col'=16] {'col'}, dimensions={0} | all-to-all | bytes 327680 | tf_op jit(solution)/shard_map/all_to_all | solution.py:140
  73.7 0.7 shard_map.50
  (1 shorter events, 0.0 us)
Async XLA Ops:
  0.0 0.7 copy-start.2
  0.7 33.8 %copy-start = (bf16[1,1,64,128,128]{4,3,2,1,0:T(8,128)(2,1)S(1)}, bf16[1,1,64,128,128]{4,3,2,1,0:T(8,128)(2,1)}, u32[]{:S(2)}) copy-start(bf16[1,1,64,128,128]{4,3,2,1,0:T(8,128)(2,1)} %blocks_ref.3) | copy-start | bytes 6291460
  0.7 33.8 %copy-start.1 = (s32[1,1,2,64]{3,2,1,0:T(2,128)S(1)}, s32[1,1,2,64]{3,2,1,0:T(2,128)}, u32[]{:S(2)}) copy-start(s32[1,1,2,64]{3,2,1,0:T(2,128)} %index_ref.3) | copy-start | bytes 1540
  33.1 3.4 %collective-permute-start = (bf16[64,8,128]{2,1,0:T(8,128)(2,1)S(1)}, bf16[64,8,128]{2,1,0:T(8,128)(2,1)S(1)}, u32[]{:S(2)}, u32[]{:S(2)}) collective-permute-start(bf16[64,8,128]{2,1,0:T(8,128)(2,1)S(1)} %all_to_all.10.near_ref), channel_id=1, source_target_pairs={{0,0},{17,1},{34,2},{51,3},{68,4},{85,5},{102,6},{119,7},{136,8},{... | collective-permute-start | bytes 393224 | tf_op jit(solution)/shard_map/ppermute | solution.py:131
  35.9 2.4 %collective-permute-start.1 = (s16[65,8,128]{2,1,0:T(8,128)(2,1)S(1)}, s16[65,8,128]{2,1,0:T(8,128)(2,1)S(1)}, u32[]{:S(2)}, u32[]{:S(2)}) collective-permute-start(s16[65,8,128]{2,1,0:T(8,128)(2,1)S(1)} %shard_map.48), channel_id=1, source_target_pairs={{0,0},{1,17},{2,34},{3,51},{4,68},{5,85},{6,102},{7,119},{8,136},{... | collective-permute-start | bytes 399368 | tf_op jit(solution)/shard_map/ppermute | solution.py:137

commit v4 on v3

--- a/solution.py
+++ b/solution.py
@@ -49,46 +49,59 @@
         out_ref[n] = own_ref[...]
 
 
-def mirrored_kernel(each, count_ref, index_ref, near_ref, blocks_ref, out_ref, sum_ref):
+def mirrored_kernel(each, count_ref, index_ref, near_ref, blocks_ref, out_ref, *sum_refs):
     off_first = lax.axis_index("col") != 0
-    sum_ref[...] = jnp.zeros_like(sum_ref)
     live = count_ref[0, 0]
-    for m in range(blocks_ref.shape[2]):
-        first = index_ref[0, 0, 0, m]
-        second = index_ref[0, 0, 1, m]
-        keep = (m < live) & (off_first | (first != second))
-        product = lax.dot_general(
-            near_ref[first], blocks_ref[0, 0, m], (((1,), (0,)), ((), ())), preferred_element_type=jnp.float32
-        )
-        sum_ref[second] = sum_ref[second] + jnp.where(keep, product, 0.0)
     chunks = out_ref.shape[0] // each
+    spare = chunks * each
+    for sum_ref in sum_refs:
+        sum_ref[...] = jnp.zeros_like(sum_ref)
+    nvec, size = near_ref.shape[1:]
+    nothing = jnp.zeros((nvec, size), near_ref.dtype)
+    for m in range(0, blocks_ref.shape[2], 2):
+        first = [index_ref[0, 0, 0, m + n] for n in range(2)]
+        second = [index_ref[0, 0, 1, m + n] for n in range(2)]
+        one, two = near_ref[first[0]], near_ref[first[1]]
+        left = jnp.concatenate([jnp.concatenate([one, nothing], 1), jnp.concatenate([nothing, two], 1)], 0)
+        right = blocks_ref[0, 0, m : m + 2].reshape(2 * size, size)
+        product = lax.dot_general(left, right, (((1,), (0,)), ((), ())), preferred_element_type=jnp.float32)
+        for n, sum_ref in enumerate(sum_refs):
+            keep = (m + n < live) & (off_first | (first[n] != second[n]))
+            goal = jnp.where(keep, second[n], spare)
+            sum_ref[goal] = sum_ref[goal] + product[n * nvec : (n + 1) * nvec]
     lane = lax.broadcasted_iota(jnp.int32, out_ref.shape[1:], 1)
     powers = jnp.zeros(out_ref.shape[1:], jnp.float32)
     for n in range(chunks):
-        codes, power = encode([sum_ref[n * each + b] for b in range(each)])
+        places = range(n * each, (n + 1) * each)
+        codes, power = encode([sum_refs[0][b] + sum_refs[1][b] for b in places])
         powers = jnp.where(lane == n, power, powers)
-        for b, code in enumerate(codes):
-            out_ref[n * each + b] = code
-    out_ref[chunks * each] = powers.astype(jnp.int32).astype(jnp.int16)
+        for b, code in zip(places, codes):
+            out_ref[b] = code
+    out_ref[spare] = powers.astype(jnp.int32).astype(jnp.int16)
 
 
-def direct_kernel(count_ref, index_ref, far_ref, blocks_ref, out_ref):
-    out_ref[...] = jnp.zeros_like(out_ref)
+def direct_kernel(count_ref, index_ref, far_ref, blocks_ref, out_ref, *sum_refs):
     live = count_ref[0, 0]
-    for m in range(blocks_ref.shape[2]):
-        first = index_ref[0, 0, 0, m]
-        second = index_ref[0, 0, 1, m]
-        product = lax.dot_general(
-            far_ref[second], blocks_ref[0, 0, m], (((1,), (1,)), ((), ())), preferred_element_type=jnp.float32
-        )
-        out_ref[first] = out_ref[first] + jnp.where(m < live, product, 0.0)
+    spare = out_ref.shape[0]
+    for sum_ref in sum_refs:
+        sum_ref[...] = jnp.zeros_like(sum_ref)
+    nvec, size = far_ref.shape[1:]
+    for m in range(0, blocks_ref.shape[2], 2):
+        left = jnp.concatenate([far_ref[index_ref[0, 0, 1, m + n]] for n in range(2)], 0)
+        right = blocks_ref[0, 0, m : m + 2].reshape(2 * size, size)
+        product = lax.dot_general(left, right, (((1,), (1,)), ((), ())), preferred_element_type=jnp.float32)
+        for n, sum_ref in enumerate(sum_refs):
+            goal = jnp.where(m + n < live, index_ref[0, 0, 0, m + n], spare)
+            sum_ref[goal] = sum_ref[goal] + product[n * nvec : (n + 1) * nvec, n * size : (n + 1) * size]
+    out_ref[...] = sum_refs[0][0:spare] + sum_refs[1][0:spare]
 
 
 def join_kernel(direct_ref, arrived_ref, out_ref):
     chunks, each = out_ref.shape[0], out_ref.shape[1] - 1
+    lane = lax.broadcasted_iota(jnp.int32, arrived_ref.shape[1:], 1)
     downs = jnp.exp2(number(arrived_ref[chunks * each]) * (1.0 / STEPS))
     for n in range(chunks):
-        down = jnp.broadcast_to(downs[:, n : n + 1], downs.shape)
+        down = jnp.sum(jnp.where(lane == n, downs, 0.0), axis=1, keepdims=True)
         sums = [direct_ref[n * each + b] + number(arrived_ref[n * each + b]) * down for b in range(each)]
         codes, power = encode(sums)
         for b, code in enumerate(codes):
@@ -130,12 +143,12 @@
     near = lax.all_to_all(copies.reshape(cols * each, nvec, size), "col", 0, 0, tiled=True)
     far = lax.ppermute(near, PLACES, joint_pairs(False))
     coded = (cols, each + 1, nvec, size)
-    sums = pltpu.VMEM(near.shape, jnp.float32)
+    sums = [pltpu.VMEM((cols * each + 1, nvec, size), jnp.float32)] * 2
     lone = (cols * each + 1, nvec, size)
     kernel = functools.partial(mirrored_kernel, each)
-    mirrored = call(kernel, lone, jnp.int16, (block_count, block_index, near, blocks), work, 2, [sums])
+    mirrored = call(kernel, lone, jnp.int16, (block_count, block_index, near, blocks), work, 1, sums)
     arrived = lax.ppermute(mirrored, PLACES, joint_pairs(True))
-    direct = call(direct_kernel, near.shape, jnp.float32, (block_count, block_index, far, blocks), 1000 * work, 2)
+    direct = call(direct_kernel, near.shape, jnp.float32, (block_count, block_index, far, blocks), 1000 * work, 1, sums)
     shares = call(join_kernel, coded, jnp.int16, (direct, arrived), work)
     shares = lax.all_to_all(shares, "col", 0, 0, tiled=True)
     total = call(total_kernel, own.shape, jnp.float32, (shares,), work)

time: 75.6 us -> 74.6 us (0.987)
  Pallas kernels: 4.31 us -> 2.43 us
  blocking collectives: 67.2 us -> 68.1 us
    pallas_call x5, Pallas kernels: 4.31 us -> 2.43 us  [call(): pl.pallas_call(kernel, out_shape=jax.ShapeDtypeStruct(out_shape, dtype),...]
    all_to_all x1, blocking collectives: 34.8 us -> 35.7 us  [per_device(): shares = lax.all_to_all(shares, 'col', 0, 0, tiled=True)]
  transfers between devices with their start and end apart: 2 -> 2, of which waited for: 0 -> 0; matrix products, arithmetic and copies ran while one was open for 0% -> 0% of each run, Pallas kernels for 4% -> 2%
where the time goes in v4:
time: 74.6 us; the launch traced here: 73.3 us
  blocking collectives  68.1 us (91%)
  Pallas kernels  2.43 us (3%)
  starting transfers between devices  1.33 us (2%)
    all_to_all x1, blocking collectives, per_device(): shares = lax.all_to_all(shares, 'col', 0, 0, tiled=True)  35.7 us
    all_to_all x1, blocking collectives, per_device(): lax.all_to_all(copies.reshape(cols * each, nvec, size), 'col', 0, 0, tile...  32.4 us
    pallas_call x5, Pallas kernels, call(): pl.pallas_call(kernel, out_shape=jax.ShapeDtypeStruct(out_shape, dtype),...  2.43 us
  transfers between devices with their start and end apart: 2, of which 0 were waited for; matrix products, arithmetic and copies ran while one was open for 0% of the time, Pallas kernels for 2%

profile of v4, /device:TPU:1, one launch (start us, length us, event | category | flops | bytes accessed | tf_op | source)
XLA Modules:
  0.0 73.3 jit_solution(17782955830596944658)
XLA Ops:
  0.0 0.0 copy-start.2
  0.0 0.7 copy-done.2
  0.7 0.0 copy-start
  0.7 0.0 copy-start.1
  0.7 32.4 %all_to_all.10.near_ref = bf16[64,8,128]{2,1,0:T(8,128)(2,1)S(1)} all-to-all(bf16[64,8,128]{2,1,0:T(8,128)(2,1)S(1)} %bitcast.7), channel_id=1, replica_groups=mesh['row'=32,'col'=16] {'col'}, dimensions={0} | all-to-all | bytes 262144 | tf_op jit(solution)/shard_map/all_to_all | solution.py:143
  33.1 0.7 collective-permute-start
  34.5 0.0 copy-done
  34.5 0.0 copy-done.1
  34.5 0.7 shard_map.48
  35.2 0.7 collective-permute-start.1
  35.8 0.0 collective-permute-done.far_ref
  35.8 0.9 %shard_map.47.direct_ref = f32[64,8,128]{2,1,0:T(8,128)S(1)} custom-call(s32[1,1]{1,0:T(1,128)S(6)} %copy.5.count_ref, s32[1,1,2,64]{3,2,1,0:T(2,128)S(1)} %copy-done.1, bf16[64,8,128]{2,1,0:T(8,128)(2,1)S(1)} %collective-permute-done.far_ref, bf16[1,1,64,128,128]{4,3,2,1,0:T(8,128)(2,1)S(1)} %copy-done), custom_call_target="tpu_custom_call" | custom-call | flops 16777216000 | bytes 1048576 | tf_op jit(solution)/shard_map/pallas_call | solution.py:124
  36.7 0.0 collective-permute-done.1.arrived_ref
  36.7 0.2 shard_map.49
  37.0 35.7 %all_to_all.11.shares_ref = s16[16,5,8,128]{3,2,1,0:T(8,128)(2,1)S(1)} all-to-all(s16[16,5,8,128]{3,2,1,0:T(8,128)(2,1)S(1)} %shard_map.49), channel_id=1, replica_groups=mesh['row'=32,'col'=16] {'col'}, dimensions={0} | all-to-all | bytes 327680 | tf_op jit(solution)/shard_map/all_to_all | solution.py:153
  72.7 0.7 shard_map.50
  (1 shorter events, 0.0 us)
Async XLA Ops:
  0.0 0.7 copy-start.2
  0.7 33.8 %copy-start = (bf16[1,1,64,128,128]{4,3,2,1,0:T(8,128)(2,1)S(1)}, bf16[1,1,64,128,128]{4,3,2,1,0:T(8,128)(2,1)}, u32[]{:S(2)}) copy-start(bf16[1,1,64,128,128]{4,3,2,1,0:T(8,128)(2,1)} %blocks_ref.3) | copy-start | bytes 6291460
  0.7 33.8 %copy-start.1 = (s32[1,1,2,64]{3,2,1,0:T(2,128)S(1)}, s32[1,1,2,64]{3,2,1,0:T(2,128)}, u32[]{:S(2)}) copy-start(s32[1,1,2,64]{3,2,1,0:T(2,128)} %index_ref.3) | copy-start | bytes 1540
  33.1 2.7 %collective-permute-start = (bf16[64,8,128]{2,1,0:T(8,128)(2,1)S(1)}, bf16[64,8,128]{2,1,0:T(8,128)(2,1)S(1)}, u32[]{:S(2)}, u32[]{:S(2)}) collective-permute-start(bf16[64,8,128]{2,1,0:T(8,128)(2,1)S(1)} %all_to_all.10.near_ref), channel_id=1, source_target_pairs={{0,0},{17,1},{34,2},{51,3},{68,4},{85,5},{102,6},{119,7},{136,8},{... | collective-permute-start | bytes 393224 | tf_op jit(solution)/shard_map/ppermute | solution.py:144
  35.2 1.6 %collective-permute-start.1 = (s16[65,8,128]{2,1,0:T(8,128)(2,1)S(1)}, s16[65,8,128]{2,1,0:T(8,128)(2,1)S(1)}, u32[]{:S(2)}, u32[]{:S(2)}) collective-permute-start(s16[65,8,128]{2,1,0:T(8,128)(2,1)S(1)} %shard_map.48), channel_id=1, source_target_pairs={{0,0},{1,17},{2,34},{3,51},{4,68},{5,85},{6,102},{7,119},{8,136},{... | collective-permute-start | bytes 399368 | tf_op jit(solution)/shard_map/ppermute | solution.py:150

commit v5 on v4

--- a/solution.py
+++ b/solution.py
@@ -11,6 +11,8 @@
 TOP = 32767.0
 STEPS = 16.0
 LEAST = 1e-33
+LEAD_IN = 10
+LEAD_OUT = 8
 
 
 def joint_pairs(to_second):
@@ -22,6 +24,12 @@
             first, second = r * cols + c, ((r + c) % rows) * cols + c
             pairs.append((first, second) if to_second else (second, first))
     return pairs
+
+
+def row_groups(lead):
+    rows = lax.axis_size("row")
+    cols = lax.axis_size("col")
+    return [[r * cols + (lead + c) % cols for c in range(cols)] for r in range(rows)]
 
 
 def encode(values):
@@ -54,6 +62,7 @@
     live = count_ref[0, 0]
     chunks = out_ref.shape[0] // each
     spare = chunks * each
+    turn = spare - LEAD_IN * each
     for sum_ref in sum_refs:
         sum_ref[...] = jnp.zeros_like(sum_ref)
     nvec, size = near_ref.shape[1:]
@@ -61,7 +70,7 @@
     for m in range(0, blocks_ref.shape[2], 2):
         first = [index_ref[0, 0, 0, m + n] for n in range(2)]
         second = [index_ref[0, 0, 1, m + n] for n in range(2)]
-        one, two = near_ref[first[0]], near_ref[first[1]]
+        one, two = [near_ref[(f + turn) % spare] for f in first]
         left = jnp.concatenate([jnp.concatenate([one, nothing], 1), jnp.concatenate([nothing, two], 1)], 0)
         right = blocks_ref[0, 0, m : m + 2].reshape(2 * size, size)
         product = lax.dot_general(left, right, (((1,), (0,)), ((), ())), preferred_element_type=jnp.float32)
@@ -80,14 +89,15 @@
     out_ref[spare] = powers.astype(jnp.int32).astype(jnp.int16)
 
 
-def direct_kernel(count_ref, index_ref, far_ref, blocks_ref, out_ref, *sum_refs):
+def direct_kernel(each, count_ref, index_ref, far_ref, blocks_ref, out_ref, *sum_refs):
     live = count_ref[0, 0]
     spare = out_ref.shape[0]
+    turn = spare - LEAD_IN * each
     for sum_ref in sum_refs:
         sum_ref[...] = jnp.zeros_like(sum_ref)
     nvec, size = far_ref.shape[1:]
     for m in range(0, blocks_ref.shape[2], 2):
-        left = jnp.concatenate([far_ref[index_ref[0, 0, 1, m + n]] for n in range(2)], 0)
+        left = jnp.concatenate([far_ref[(index_ref[0, 0, 1, m + n] + turn) % spare] for n in range(2)], 0)
         right = blocks_ref[0, 0, m : m + 2].reshape(2 * size, size)
         product = lax.dot_general(left, right, (((1,), (1,)), ((), ())), preferred_element_type=jnp.float32)
         for n, sum_ref in enumerate(sum_refs):
@@ -104,9 +114,10 @@
         down = jnp.sum(jnp.where(lane == n, downs, 0.0), axis=1, keepdims=True)
         sums = [direct_ref[n * each + b] + number(arrived_ref[n * each + b]) * down for b in range(each)]
         codes, power = encode(sums)
+        place = (n - LEAD_OUT) % chunks
         for b, code in enumerate(codes):
-            out_ref[n, b] = code
-        out_ref[n, each] = power.astype(jnp.int32).astype(jnp.int16)
+            out_ref[place, b] = code
+        out_ref[place, each] = power.astype(jnp.int32).astype(jnp.int16)
 
 
 def total_kernel(shares_ref, out_ref):
@@ -140,7 +151,8 @@
     work = 2 * nvec * blocks.size
     own = vectors.reshape(nvec, each, size).transpose(1, 0, 2)
     copies = call(spread_kernel, (cols,) + own.shape, own.dtype, (own,), 1000 * work)
-    near = lax.all_to_all(copies.reshape(cols * each, nvec, size), "col", 0, 0, tiled=True)
+    copies = copies.reshape(cols * each, nvec, size)
+    near = lax.all_to_all(copies, PLACES, 0, 0, axis_index_groups=row_groups(LEAD_IN), tiled=True)
     far = lax.ppermute(near, PLACES, joint_pairs(False))
     coded = (cols, each + 1, nvec, size)
     sums = [pltpu.VMEM((cols * each + 1, nvec, size), jnp.float32)] * 2
@@ -148,9 +160,10 @@
     kernel = functools.partial(mirrored_kernel, each)
     mirrored = call(kernel, lone, jnp.int16, (block_count, block_index, near, blocks), work, 1, sums)
     arrived = lax.ppermute(mirrored, PLACES, joint_pairs(True))
-    direct = call(direct_kernel, near.shape, jnp.float32, (block_count, block_index, far, blocks), 1000 * work, 1, sums)
+    kernel = functools.partial(direct_kernel, each)
+    direct = call(kernel, near.shape, jnp.float32, (block_count, block_index, far, blocks), 1000 * work, 1, sums)
     shares = call(join_kernel, coded, jnp.int16, (direct, arrived), work)
-    shares = lax.all_to_all(shares, "col", 0, 0, tiled=True)
+    shares = lax.all_to_all(shares, PLACES, 0, 0, axis_index_groups=row_groups(LEAD_OUT), tiled=True)
     total = call(total_kernel, own.shape, jnp.float32, (shares,), work)
     return total.transpose(1, 0, 2).reshape(nvec, width)
 

time: 74.6 us -> 67.9 us (0.910); the launches traced: 73.3 us -> 67.6 us
  blocking collectives: 68.1 us -> 62.3 us
    all_to_all x2, blocking collectives: 68.1 us -> 62.3 us  [the longest x1 36.7 us: per_device(): lax.all_to_all(shares, PLACES, 0, 0, axis_index_groups=row_groups(LEAD_OU...]
where the time goes in v5:
time: 67.9 us; the launch traced here: 67.6 us
  blocking collectives  62.3 us (92%)
  Pallas kernels  2.53 us (4%)
  starting transfers between devices  1.33 us (2%)
  between operations  0.72 us (1%)
  local copies, waits for them, and re-layouts  0.7 us (1%)
    all_to_all x1, blocking collectives, per_device(): lax.all_to_all(shares, PLACES, 0, 0, axis_index_groups=row_groups(LEAD_OU...  36.7 us
    all_to_all x1, blocking collectives, per_device(): lax.all_to_all(copies, PLACES, 0, 0, axis_index_groups=row_groups(LEAD_IN...  25.7 us
    pallas_call x5, Pallas kernels, call(): pl.pallas_call(kernel, out_shape=jax.ShapeDtypeStruct(out_shape, dtype),...  2.53 us
  transfers between devices with their start and end apart: 2, of which 0 were waited for; matrix products, arithmetic and copies ran while one was open for 0% of the time, Pallas kernels for 2%

profile of v5, /device:TPU:1, one launch (start us, length us, event | category | flops | bytes accessed | tf_op | source)
XLA Modules:
  0.0 67.6 jit_solution(10551092833220981664)
XLA Ops:
  0.0 0.0 copy-start.2
  0.0 0.7 %copy-done.2 = bf16[8,512]{1,0:T(8,128)(2,1)S(1)} copy-done((bf16[8,512]{1,0:T(8,128)(2,1)S(1)}, bf16[8,512]{1,0:T(8,128)(2,1)}, u32[]{:S(2)}) %copy-start.2) | copy-done | bytes 8216
  0.7 0.0 copy-start
  0.7 0.0 copy-start.1
  0.7 25.7 %all_to_all.10.near_ref = bf16[64,8,128]{2,1,0:T(8,128)(2,1)S(1)} all-to-all(bf16[64,8,128]{2,1,0:T(8,128)(2,1)S(1)} %bitcast.7), channel_id=1, replica_groups={{10,11,12,13,14,15,0,1,2,3,4,5,6,7,8,9},{26,27,28,29,30,31,16,17,18,19,..., dimensions={0} | all-to-all | bytes 262144 | tf_op jit(solution)/shard_map/all_to_all | solution.py:155
  26.4 0.7 collective-permute-start
  27.7 0.0 copy-done
  27.7 0.0 copy-done.1
  27.7 0.8 %shard_map.48 = s16[65,8,128]{2,1,0:T(8,128)(2,1)S(1)} custom-call(s32[1,1]{1,0:T(1,128)S(6)} %copy.5.count_ref, s32[1,1,2,64]{3,2,1,0:T(2,128)S(1)} %copy-done.1, bf16[64,8,128]{2,1,0:T(8,128)(2,1)S(1)} %all_to_all.10.near_ref, bf16[1,1,64,128,128]{4,3,2,1,0:T(8,128)(2,1)S(1)} %copy-done), custom_call_target="tpu_custom_call" | custom-call | flops 16777216 | bytes 1048576 | tf_op jit(solution)/shard_map/pallas_call | solution.py:135
  28.5 0.7 collective-permute-start.1
  29.2 0.0 collective-permute-done.far_ref
  29.2 0.8 %shard_map.47.direct_ref = f32[64,8,128]{2,1,0:T(8,128)S(1)} custom-call(s32[1,1]{1,0:T(1,128)S(6)} %copy.5.count_ref, s32[1,1,2,64]{3,2,1,0:T(2,128)S(1)} %copy-done.1, bf16[64,8,128]{2,1,0:T(8,128)(2,1)S(1)} %collective-permute-done.far_ref, bf16[1,1,64,128,128]{4,3,2,1,0:T(8,128)(2,1)S(1)} %copy-done), custom_call_target="tpu_custom_call" | custom-call | flops 16777216000 | bytes 1048576 | tf_op jit(solution)/shard_map/pallas_call | solution.py:135
  30.0 0.0 collective-permute-done.1.arrived_ref
  30.1 0.2 shard_map.49
  30.3 36.7 %all_to_all.11.shares_ref = s16[16,5,8,128]{3,2,1,0:T(8,128)(2,1)S(1)} all-to-all(s16[16,5,8,128]{3,2,1,0:T(8,128)(2,1)S(1)} %shard_map.49), channel_id=1, replica_groups={{8,9,10,11,12,13,14,15,0,1,2,3,4,5,6,7},{24,25,26,27,28,29,30,31,16,17,..., dimensions={0} | all-to-all | bytes 327680 | tf_op jit(solution)/shard_map/all_to_all | solution.py:166
  67.0 0.7 shard_map.50
  (1 shorter events, 0.0 us)
Async XLA Ops:
  0.0 0.7 %copy-start.2 = (bf16[8,512]{1,0:T(8,128)(2,1)S(1)}, bf16[8,512]{1,0:T(8,128)(2,1)}, u32[]{:S(2)}) copy-start(bf16[8,512]{1,0:T(8,128)(2,1)} %param.4) | copy-start | bytes 24580
  0.7 27.0 %copy-start = (bf16[1,1,64,128,128]{4,3,2,1,0:T(8,128)(2,1)S(1)}, bf16[1,1,64,128,128]{4,3,2,1,0:T(8,128)(2,1)}, u32[]{:S(2)}) copy-start(bf16[1,1,64,128,128]{4,3,2,1,0:T(8,128)(2,1)} %blocks_ref.3) | copy-start | bytes 6291460
  0.7 27.0 %copy-start.1 = (s32[1,1,2,64]{3,2,1,0:T(2,128)S(1)}, s32[1,1,2,64]{3,2,1,0:T(2,128)}, u32[]{:S(2)}) copy-start(s32[1,1,2,64]{3,2,1,0:T(2,128)} %index_ref.3) | copy-start | bytes 1540
  26.4 2.8 %collective-permute-start = (bf16[64,8,128]{2,1,0:T(8,128)(2,1)S(1)}, bf16[64,8,128]{2,1,0:T(8,128)(2,1)S(1)}, u32[]{:S(2)}, u32[]{:S(2)}) collective-permute-start(bf16[64,8,128]{2,1,0:T(8,128)(2,1)S(1)} %all_to_all.10.near_ref), channel_id=1, source_target_pairs={{0,0},{17,1},{34,2},{51,3},{68,4},{85,5},{102,6},{119,7},{136,8},{... | collective-permute-start | bytes 393224 | tf_op jit(solution)/shard_map/ppermute | solution.py:156
  28.5 1.5 %collective-permute-start.1 = (s16[65,8,128]{2,1,0:T(8,128)(2,1)S(1)}, s16[65,8,128]{2,1,0:T(8,128)(2,1)S(1)}, u32[]{:S(2)}, u32[]{:S(2)}) collective-permute-start(s16[65,8,128]{2,1,0:T(8,128)(2,1)S(1)} %shard_map.48), channel_id=1, source_target_pairs={{0,0},{1,17},{2,34},{3,51},{4,68},{5,85},{6,102},{7,119},{8,136},{... | collective-permute-start | bytes 399368 | tf_op jit(solution)/shard_map/ppermute | solution.py:162

commit v6 on v5

--- a/solution.py
+++ b/solution.py
@@ -11,8 +11,8 @@
 TOP = 32767.0
 STEPS = 16.0
 LEAST = 1e-33
-LEAD_IN = 10
-LEAD_OUT = 8
+LEAD_IN = 9
+LEAD_OUT = 10
 
 
 def joint_pairs(to_second):

time: 67.9 us -> 67 us (0.987)
  blocking collectives: 62.3 us -> 61.4 us
    all_to_all x1, blocking collectives: 36.7 us -> 34.8 us  [per_device(): lax.all_to_all(shares, PLACES, 0, 0, axis_index_groups=row_groups(LEAD_OU...]
    all_to_all x1, blocking collectives: 25.7 us -> 26.6 us  [per_device(): lax.all_to_all(copies, PLACES, 0, 0, axis_index_groups=row_groups(LEAD_IN...]
where the time goes in v6:
time: 67 us; the launch traced here: 66.7 us
  blocking collectives  61.4 us (92%)
  Pallas kernels  2.52 us (4%)
  starting transfers between devices  1.33 us (2%)
  between operations  0.72 us (1%)
  local copies, waits for them, and re-layouts  0.7 us (1%)
    all_to_all x1, blocking collectives, per_device(): lax.all_to_all(shares, PLACES, 0, 0, axis_index_groups=row_groups(LEAD_OU...  34.8 us
    all_to_all x1, blocking collectives, per_device(): lax.all_to_all(copies, PLACES, 0, 0, axis_index_groups=row_groups(LEAD_IN...  26.6 us
    pallas_call x5, Pallas kernels, call(): pl.pallas_call(kernel, out_shape=jax.ShapeDtypeStruct(out_shape, dtype),...  2.52 us
  transfers between devices with their start and end apart: 2, of which 0 were waited for; matrix products, arithmetic and copies ran while one was open for 0% of the time, Pallas kernels for 2%

profile of v6, /device:TPU:1, one launch (start us, length us, event | category | flops | bytes accessed | tf_op | source)
XLA Modules:
  0.0 66.7 jit_solution(327117114346015197)
XLA Ops:
  0.0 0.0 copy-start.2
  0.0 0.7 %copy-done.2 = bf16[8,512]{1,0:T(8,128)(2,1)S(1)} copy-done((bf16[8,512]{1,0:T(8,128)(2,1)S(1)}, bf16[8,512]{1,0:T(8,128)(2,1)}, u32[]{:S(2)}) %copy-start.2) | copy-done | bytes 8216
  0.7 0.0 copy-start
  0.7 0.0 copy-start.1
  0.7 26.6 %all_to_all.10.near_ref = bf16[64,8,128]{2,1,0:T(8,128)(2,1)S(1)} all-to-all(bf16[64,8,128]{2,1,0:T(8,128)(2,1)S(1)} %bitcast.7), channel_id=1, replica_groups={{9,10,11,12,13,14,15,0,1,2,3,4,5,6,7,8},{25,26,27,28,29,30,31,16,17,18,..., dimensions={0} | all-to-all | bytes 262144 | tf_op jit(solution)/shard_map/all_to_all | solution.py:155
  27.4 0.7 collective-permute-start
  28.7 0.0 copy-done
  28.7 0.0 copy-done.1
  28.7 0.8 %shard_map.48 = s16[65,8,128]{2,1,0:T(8,128)(2,1)S(1)} custom-call(s32[1,1]{1,0:T(1,128)S(6)} %copy.5.count_ref, s32[1,1,2,64]{3,2,1,0:T(2,128)S(1)} %copy-done.1, bf16[64,8,128]{2,1,0:T(8,128)(2,1)S(1)} %all_to_all.10.near_ref, bf16[1,1,64,128,128]{4,3,2,1,0:T(8,128)(2,1)S(1)} %copy-done), custom_call_target="tpu_custom_call" | custom-call | flops 16777216 | bytes 1048576 | tf_op jit(solution)/shard_map/pallas_call | solution.py:135
  29.5 0.7 %collective-permute-start.1 = (s16[65,8,128]{2,1,0:T(8,128)(2,1)S(1)}, s16[65,8,128]{2,1,0:T(8,128)(2,1)S(1)}, u32[]{:S(2)}, u32[]{:S(2)}) collective-permute-start(s16[65,8,128]{2,1,0:T(8,128)(2,1)S(1)} %shard_map.48), channel_id=1, source_target_pairs={{0,0},{1,17},{2,34},{3,51},{4,68},{5,85},{6,102},{7,119},{8,136},{... | collective-permute-start | bytes 399368 | tf_op jit(solution)/shard_map/ppermute | solution.py:162
  30.2 0.0 collective-permute-done.far_ref
  30.2 0.8 %shard_map.47.direct_ref = f32[64,8,128]{2,1,0:T(8,128)S(1)} custom-call(s32[1,1]{1,0:T(1,128)S(6)} %copy.5.count_ref, s32[1,1,2,64]{3,2,1,0:T(2,128)S(1)} %copy-done.1, bf16[64,8,128]{2,1,0:T(8,128)(2,1)S(1)} %collective-permute-done.far_ref, bf16[1,1,64,128,128]{4,3,2,1,0:T(8,128)(2,1)S(1)} %copy-done), custom_call_target="tpu_custom_call" | custom-call | flops 16777216000 | bytes 1048576 | tf_op jit(solution)/shard_map/pallas_call | solution.py:135
  31.0 0.0 collective-permute-done.1.arrived_ref
  31.0 0.2 shard_map.49
  31.3 34.8 %all_to_all.11.shares_ref = s16[16,5,8,128]{3,2,1,0:T(8,128)(2,1)S(1)} all-to-all(s16[16,5,8,128]{3,2,1,0:T(8,128)(2,1)S(1)} %shard_map.49), channel_id=1, replica_groups={{10,11,12,13,14,15,0,1,2,3,4,5,6,7,8,9},{26,27,28,29,30,31,16,17,18,19,..., dimensions={0} | all-to-all | bytes 327680 | tf_op jit(solution)/shard_map/all_to_all | solution.py:166
  66.0 0.7 shard_map.50
  (1 shorter events, 0.0 us)
Async XLA Ops:
  0.0 0.7 %copy-start.2 = (bf16[8,512]{1,0:T(8,128)(2,1)S(1)}, bf16[8,512]{1,0:T(8,128)(2,1)}, u32[]{:S(2)}) copy-start(bf16[8,512]{1,0:T(8,128)(2,1)} %param.4) | copy-start | bytes 24580
  0.7 28.0 %copy-start = (bf16[1,1,64,128,128]{4,3,2,1,0:T(8,128)(2,1)S(1)}, bf16[1,1,64,128,128]{4,3,2,1,0:T(8,128)(2,1)}, u32[]{:S(2)}) copy-start(bf16[1,1,64,128,128]{4,3,2,1,0:T(8,128)(2,1)} %blocks_ref.3) | copy-start | bytes 6291460
  0.7 28.0 %copy-start.1 = (s32[1,1,2,64]{3,2,1,0:T(2,128)S(1)}, s32[1,1,2,64]{3,2,1,0:T(2,128)}, u32[]{:S(2)}) copy-start(s32[1,1,2,64]{3,2,1,0:T(2,128)} %index_ref.3) | copy-start | bytes 1540
  27.4 2.8 %collective-permute-start = (bf16[64,8,128]{2,1,0:T(8,128)(2,1)S(1)}, bf16[64,8,128]{2,1,0:T(8,128)(2,1)S(1)}, u32[]{:S(2)}, u32[]{:S(2)}) collective-permute-start(bf16[64,8,128]{2,1,0:T(8,128)(2,1)S(1)} %all_to_all.10.near_ref), channel_id=1, source_target_pairs={{0,0},{17,1},{34,2},{51,3},{68,4},{85,5},{102,6},{119,7},{136,8},{... | collective-permute-start | bytes 393224 | tf_op jit(solution)/shard_map/ppermute | solution.py:156
  29.5 1.5 %collective-permute-start.1 = (s16[65,8,128]{2,1,0:T(8,128)(2,1)S(1)}, s16[65,8,128]{2,1,0:T(8,128)(2,1)S(1)}, u32[]{:S(2)}, u32[]{:S(2)}) collective-permute-start(s16[65,8,128]{2,1,0:T(8,128)(2,1)S(1)} %shard_map.48), channel_id=1, source_target_pairs={{0,0},{1,17},{2,34},{3,51},{4,68},{5,85},{6,102},{7,119},{8,136},{... | collective-permute-start | bytes 399368 | tf_op jit(solution)/shard_map/ppermute | solution.py:162

commit v7 on v6

--- a/solution.py
+++ b/solution.py
@@ -11,7 +11,7 @@
 TOP = 32767.0
 STEPS = 16.0
 LEAST = 1e-33
-LEAD_IN = 9
+LEAD_IN = 8
 LEAD_OUT = 10
 
 
@@ -70,7 +70,7 @@
     for m in range(0, blocks_ref.shape[2], 2):
         first = [index_ref[0, 0, 0, m + n] for n in range(2)]
         second = [index_ref[0, 0, 1, m + n] for n in range(2)]
-        one, two = [near_ref[(f + turn) % spare] for f in first]
+        one, two = [near_ref[(f + turn) & (spare - 1)] for f in first]
         left = jnp.concatenate([jnp.concatenate([one, nothing], 1), jnp.concatenate([nothing, two], 1)], 0)
         right = blocks_ref[0, 0, m : m + 2].reshape(2 * size, size)
         product = lax.dot_general(left, right, (((1,), (0,)), ((), ())), preferred_element_type=jnp.float32)
@@ -97,7 +97,7 @@
         sum_ref[...] = jnp.zeros_like(sum_ref)
     nvec, size = far_ref.shape[1:]
     for m in range(0, blocks_ref.shape[2], 2):
-        left = jnp.concatenate([far_ref[(index_ref[0, 0, 1, m + n] + turn) % spare] for n in range(2)], 0)
+        left = jnp.concatenate([far_ref[(index_ref[0, 0, 1, m + n] + turn) & (spare - 1)] for n in range(2)], 0)
         right = blocks_ref[0, 0, m : m + 2].reshape(2 * size, size)
         product = lax.dot_general(left, right, (((1,), (1,)), ((), ())), preferred_element_type=jnp.float32)
         for n, sum_ref in enumerate(sum_refs):

time: 67 us -> 66.4 us (level)
  blocking collectives: 61.4 us -> 60.6 us
    all_to_all x1, blocking collectives: 34.8 us -> 33.2 us  [per_device(): lax.all_to_all(shares, PLACES, 0, 0, axis_index_groups=row_groups(LEAD_OU...]
    all_to_all x1, blocking collectives: 26.6 us -> 27.4 us  [per_device(): lax.all_to_all(copies, PLACES, 0, 0, axis_index_groups=row_groups(LEAD_IN...]
where the time goes in v7:
time: 66.4 us; the launch traced here: 65.8 us
  blocking collectives  60.6 us (91%)
  Pallas kernels  2.43 us (4%)
  starting transfers between devices  1.33 us (2%)
  between operations  0.72 us (1%)
  local copies, waits for them, and re-layouts  0.7 us (1%)
    all_to_all x1, blocking collectives, per_device(): lax.all_to_all(shares, PLACES, 0, 0, axis_index_groups=row_groups(LEAD_OU...  33.2 us
    all_to_all x1, blocking collectives, per_device(): lax.all_to_all(copies, PLACES, 0, 0, axis_index_groups=row_groups(LEAD_IN...  27.4 us
    pallas_call x5, Pallas kernels, call(): pl.pallas_call(kernel, out_shape=jax.ShapeDtypeStruct(out_shape, dtype),...  2.43 us
  transfers between devices with their start and end apart: 2, of which 0 were waited for; matrix products, arithmetic and copies ran while one was open for 0% of the time, Pallas kernels for 2%

profile of v7, /device:TPU:1, one launch (start us, length us, event | category | flops | bytes accessed | tf_op | source)
XLA Modules:
  0.0 65.8 jit_solution(16458225287578070040)
XLA Ops:
  0.0 0.0 copy-start.2
  0.0 0.7 %copy-done.2 = bf16[8,512]{1,0:T(8,128)(2,1)S(1)} copy-done((bf16[8,512]{1,0:T(8,128)(2,1)S(1)}, bf16[8,512]{1,0:T(8,128)(2,1)}, u32[]{:S(2)}) %copy-start.2) | copy-done | bytes 8216
  0.7 0.0 copy-start
  0.7 0.0 copy-start.1
  0.7 27.4 %all_to_all.10.near_ref = bf16[64,8,128]{2,1,0:T(8,128)(2,1)S(1)} all-to-all(bf16[64,8,128]{2,1,0:T(8,128)(2,1)S(1)} %bitcast.7), channel_id=1, replica_groups={{8,9,10,11,12,13,14,15,0,1,2,3,4,5,6,7},{24,25,26,27,28,29,30,31,16,17,..., dimensions={0} | all-to-all | bytes 262144 | tf_op jit(solution)/shard_map/all_to_all | solution.py:155
  28.1 0.7 collective-permute-start
  29.5 0.0 copy-done
  29.5 0.0 copy-done.1
  29.5 0.7 %shard_map.48 = s16[65,8,128]{2,1,0:T(8,128)(2,1)S(1)} custom-call(s32[1,1]{1,0:T(1,128)S(6)} %copy.5.count_ref, s32[1,1,2,64]{3,2,1,0:T(2,128)S(1)} %copy-done.1, bf16[64,8,128]{2,1,0:T(8,128)(2,1)S(1)} %all_to_all.10.near_ref, bf16[1,1,64,128,128]{4,3,2,1,0:T(8,128)(2,1)S(1)} %copy-done), custom_call_target="tpu_custom_call" | custom-call | flops 16777216 | bytes 1048576 | tf_op jit(solution)/shard_map/pallas_call | solution.py:135
  30.1 0.7 %collective-permute-start.1 = (s16[65,8,128]{2,1,0:T(8,128)(2,1)S(1)}, s16[65,8,128]{2,1,0:T(8,128)(2,1)S(1)}, u32[]{:S(2)}, u32[]{:S(2)}) collective-permute-start(s16[65,8,128]{2,1,0:T(8,128)(2,1)S(1)} %shard_map.48), channel_id=1, source_target_pairs={{0,0},{1,17},{2,34},{3,51},{4,68},{5,85},{6,102},{7,119},{8,136},{... | collective-permute-start | bytes 399368 | tf_op jit(solution)/shard_map/ppermute | solution.py:162
  30.8 0.0 collective-permute-done.far_ref
  30.8 0.8 %shard_map.47.direct_ref = f32[64,8,128]{2,1,0:T(8,128)S(1)} custom-call(s32[1,1]{1,0:T(1,128)S(6)} %copy.5.count_ref, s32[1,1,2,64]{3,2,1,0:T(2,128)S(1)} %copy-done.1, bf16[64,8,128]{2,1,0:T(8,128)(2,1)S(1)} %collective-permute-done.far_ref, bf16[1,1,64,128,128]{4,3,2,1,0:T(8,128)(2,1)S(1)} %copy-done), custom_call_target="tpu_custom_call" | custom-call | flops 16777216000 | bytes 1048576 | tf_op jit(solution)/shard_map/pallas_call | solution.py:135
  31.7 0.0 collective-permute-done.1.arrived_ref
  31.7 0.2 shard_map.49
  31.9 33.2 %all_to_all.11.shares_ref = s16[16,5,8,128]{3,2,1,0:T(8,128)(2,1)S(1)} all-to-all(s16[16,5,8,128]{3,2,1,0:T(8,128)(2,1)S(1)} %shard_map.49), channel_id=1, replica_groups={{10,11,12,13,14,15,0,1,2,3,4,5,6,7,8,9},{26,27,28,29,30,31,16,17,18,19,..., dimensions={0} | all-to-all | bytes 327680 | tf_op jit(solution)/shard_map/all_to_all | solution.py:166
  65.2 0.7 shard_map.50
  (1 shorter events, 0.0 us)
Async XLA Ops:
  0.0 0.7 %copy-start.2 = (bf16[8,512]{1,0:T(8,128)(2,1)S(1)}, bf16[8,512]{1,0:T(8,128)(2,1)}, u32[]{:S(2)}) copy-start(bf16[8,512]{1,0:T(8,128)(2,1)} %param.4) | copy-start | bytes 24580
  0.7 28.8 %copy-start = (bf16[1,1,64,128,128]{4,3,2,1,0:T(8,128)(2,1)S(1)}, bf16[1,1,64,128,128]{4,3,2,1,0:T(8,128)(2,1)}, u32[]{:S(2)}) copy-start(bf16[1,1,64,128,128]{4,3,2,1,0:T(8,128)(2,1)} %blocks_ref.3) | copy-start | bytes 6291460
  0.7 28.8 %copy-start.1 = (s32[1,1,2,64]{3,2,1,0:T(2,128)S(1)}, s32[1,1,2,64]{3,2,1,0:T(2,128)}, u32[]{:S(2)}) copy-start(s32[1,1,2,64]{3,2,1,0:T(2,128)} %index_ref.3) | copy-start | bytes 1540
  28.1 2.7 %collective-permute-start = (bf16[64,8,128]{2,1,0:T(8,128)(2,1)S(1)}, bf16[64,8,128]{2,1,0:T(8,128)(2,1)S(1)}, u32[]{:S(2)}, u32[]{:S(2)}) collective-permute-start(bf16[64,8,128]{2,1,0:T(8,128)(2,1)S(1)} %all_to_all.10.near_ref), channel_id=1, source_target_pairs={{0,0},{17,1},{34,2},{51,3},{68,4},{85,5},{102,6},{119,7},{136,8},{... | collective-permute-start | bytes 393224 | tf_op jit(solution)/shard_map/ppermute | solution.py:156
  30.1 1.5 %collective-permute-start.1 = (s16[65,8,128]{2,1,0:T(8,128)(2,1)S(1)}, s16[65,8,128]{2,1,0:T(8,128)(2,1)S(1)}, u32[]{:S(2)}, u32[]{:S(2)}) collective-permute-start(s16[65,8,128]{2,1,0:T(8,128)(2,1)S(1)} %shard_map.48), channel_id=1, source_target_pairs={{0,0},{1,17},{2,34},{3,51},{4,68},{5,85},{6,102},{7,119},{8,136},{... | collective-permute-start | bytes 399368 | tf_op jit(solution)/shard_map/ppermute | solution.py:162
